TPU v7x, 128 devices: a whole 4x4x4 slice. The times are simulated.
128 devices in a mesh: grp: 32 (over x, y, core), blk: 4 (over z).
Axes of the slice: x: 4, y: 4, z: 4, core: 2. Of those that a mesh axis runs over, the one named last changes fastest.
Arguments:
- embeddings: bfloat16 [65536, 1024], P(('grp', 'blk'))
- cluster_ids: int32 [65536, 1], P(('grp', 'blk')), may hold values from 0 to 31; in each aligned block of 512 rows (0 to 511, 512 to 1023, ...) at most 64 rows name the same one
- priority: int32 [65536], P(('grp', 'blk')), may hold values from 0 to 65535, each once
Outputs:
- best_match: float32 [65536], P(('grp', 'blk'))
Inputs may be any that keep to these rules, and one draw needn't show every extreme that they name: `cluster_ids`: the 512 rows of one device name one cluster at most 64 times, a bound that some block reaches.
All inputs are finite; a program needn't handle non-finite values.
Results may differ from a plain program's by a relative error of at most 0.00049.
Values may be sent and summed in bfloat16 or wider, within the bound.
A program may use at most 128 MiB of HBM per device.

v0:
```python
import jax
import jax.numpy as jnp
from jax import lax
from jax.sharding import PartitionSpec as P

SLOT = 64
never_rank = 2**30


def local(embeddings, cluster_ids, priority):
    width = embeddings.shape[1]
    groups = lax.axis_size("grp")
    slots = SLOT
    wide = embeddings.astype(jnp.float32)
    unit = (wide / jnp.sqrt(jnp.sum(wide * wide, axis=1, keepdims=True) + 1e-06)).astype(
        jnp.bfloat16
    )
    labels = cluster_ids[:, 0]
    onehot = (labels[:, None] == jnp.arange(groups, dtype=jnp.int32)[None, :]).astype(jnp.int32)
    before = jnp.cumsum(onehot, axis=0) - onehot
    position = jnp.sum(onehot * before, axis=1)
    target = labels * slots + position
    outbox = jnp.zeros((groups * slots, width), jnp.bfloat16).at[target].set(unit)
    outrank = jnp.full((groups * slots,), never_rank, jnp.int32).at[target].set(priority)
    inbox, inrank = (
        lax.all_to_all(
            outbox.reshape(groups, slots, width), "grp", split_axis=0, concat_axis=0, tiled=True
        ),
        lax.all_to_all(
            outrank.reshape(groups, slots), "grp", split_axis=0, concat_axis=0, tiled=True
        ),
    )
    query = inbox.reshape(groups * slots, width)
    q_rank = inrank.reshape(groups * slots)
    local_rows = groups * slots
    start_best = jnp.full((local_rows,), -1.0, jnp.float32)
    scores = lax.dot_general(
        query,
        lax.all_gather(query, "blk", axis=0, tiled=True),
        (((1,), (1,)), ((), ())),
        preferred_element_type=jnp.float32,
    )
    allowed = lax.all_gather(q_rank, "blk", axis=0, tiled=True)[None, :] < q_rank[:, None]
    best_local = jnp.maximum(
        start_best, jnp.max(jnp.where(allowed, scores, jnp.float32(-1.0)), axis=1)
    )
    returned = lax.all_to_all(
        best_local.reshape(groups, slots), "grp", split_axis=0, concat_axis=0, tiled=True
    )
    return returned.reshape(groups * slots)[target]


def solution(mesh):
    placed = (P(("grp", "blk"), None), P(("grp", "blk"), None), P(("grp", "blk")))
    return jax.shard_map(
        local, mesh=mesh, in_specs=placed, out_specs=P(("grp", "blk")), check_vma=False
    )
```

profile of v0, /device:TPU:1, one launch (start us, length us, event | category | flops | bytes accessed | tf_op | source)
XLA Modules:
  0.0 297.9 jit_solution(7682525953630342940)
XLA Ops:
  6.5 0.7 fusion.9
  7.2 1.2 reduce-window.6
  8.4 0.2 slice_reduce_fusion
  8.6 0.8 fusion.8
  9.4 0.7 compare_select_fusion
  10.1 1.5 fusion
  11.6 6.0 %scatter_custom_fusion.1 = bf16[2048,1024]{1,0:T(8,128)(2,1)} fusion(s32[512]{0:T(512)S(1)} %bitcast.32, bf16[]{:T(256)} %constant.4.clone.1, bf16[512,1024]{1,0:T(8,128)(2,1)} %param.3, f32[512]{0:T(512)S(1)} %add_sqrt_fusion), kind=kCustom, calls=%fused_computation.8 | custom fusion | flops 1572864 | bytes 5244930 | tf_op jit(solution)/shard_map/scatter | solution.py:23
  17.6 59.3 %all_to_all.20 = bf16[32,64,1024]{2,1,0:T(8,128)(2,1)} all-to-all(bf16[32,64,1024]{2,1,0:T(8,128)(2,1)} %bitcast.27), channel_id=1, replica_groups=mesh['grp'=32,'blk'=4] {'grp'}, dimensions={0} | all-to-all | bytes 8388608 | tf_op jit(solution)/shard_map/all_to_all | solution.py:26
  76.9 2.6 scatter_custom_fusion
  79.5 0.1 all_to_all.13
  79.6 10.7 %all_to_all.21 = s32[32,1,64]{2,1,0:T(1,128)S(1)} all-to-all(s32[32,1,64]{2,1,0:T(1,128)S(1)} %all_to_all.13), channel_id=1, replica_groups=mesh['grp'=32,'blk'=4] {'grp'}, dimensions={0} | all-to-all | bytes 16384 | tf_op jit(solution)/shard_map/all_to_all | solution.py:29
  90.3 0.5 broadcast.58
  90.8 0.7 reduce.8
  91.5 0.1 reshape.61
  91.6 11.5 %all_gather.6 = s32[8192]{0:T(1024)S(1)} all-gather(s32[2048]{0:T(1024)S(1)} %reshape.61), channel_id=1, replica_groups=mesh['grp'=32,'blk'=4] {'blk'}, dimensions={0}, use_global_device_ids=true | all-gather | bytes 40960 | tf_op jit(solution)/shard_map/all_gather | solution.py:43
  103.1 127.0 %all-gather.2.cloned.1.call-done = bf16[8192,1024]{1,0:T(8,128)(2,1)} async-done(((bf16[2048,1024]{1,0:T(8,128)(2,1)}), bf16[8192,1024]{1,0:T(8,128)(2,1)}) %all-gather.2.cloned.1.call-update) | async-done | bytes 16777232 | tf_op jit(solution)/shard_map/all_gather | solution.py:39
  230.1 40.3 %select_reduce_fusion = f32[2048]{0:T(1024)S(1)} fusion(bf16[2048,1024]{1,0:T(8,128)(2,1)} %bitcast.29, bf16[8192,1024]{1,0:T(8,128)(2,1)} %all-gather.2.cloned.1.call-done, s32[8192]{0:T(1024)S(1)} %all_gather.6, s32[2048]{0:T(1024)S(1)} %reshape.61), kind=kOutput, calls=%fused_computation.3 | convolution fusion | flops 34410070016 | bytes 21020672 | tf_op jit(solution)/shard_map/dot_general | solution.py:37
  270.4 0.7 max_broadcast_in_dim.15
  271.1 7.5 %all-to-all-start.2 = ((f32[32,1,64]{2,1,0:T(1,128)}), f32[32,1,64]{2,1,0:T(1,128)S(1)}, u32[]{:S(2)}, u32[]{:S(2)}) async-start(f32[32,1,64]{2,1,0:T(1,128)} %max_broadcast_in_dim.15), calls=%async_computation.2 | async-start | bytes 32768 | tf_op jit(solution)/shard_map/all_to_all | solution.py:47
  278.5 6.9 %all-to-all-done.2 = f32[32,1,64]{2,1,0:T(1,128)S(1)} async-done(((f32[32,1,64]{2,1,0:T(1,128)}), f32[32,1,64]{2,1,0:T(1,128)S(1)}, u32[]{:S(2)}, u32[]{:S(2)}) %all-to-all-start.2) | async-done | bytes 8224 | tf_op jit(solution)/shard_map/all_to_all | solution.py:47
  285.5 0.5 broadcast.59
  286.0 0.7 reduce.9
  286.7 0.1 reshape.64
  286.7 4.3 %gather_fusion = f32[512]{0:T(512)} fusion(f32[2048]{0:T(1024)S(1)} %reshape.64, s32[1024]{0:T(1024)S(1)} %pad_clamp_fusion), kind=kCustom, calls=%fused_computation | custom fusion | bytes 6144 | tf_op jit(solution)/shard_map/gather | solution.py:50
  (7 shorter events, 0.1 us)
Async XLA Ops:
  6.5 223.5 %all-gather.2.cloned.1.call-start = ((), (), s32[]{:S(2)}) async-start(), calls=%async_computation.3 | async-start | bytes 20971520 | tf_op jit(solution)/shard_map/all_gather | solution.py:39
  271.1 14.4 %all-to-all-start.2 = ((f32[32,1,64]{2,1,0:T(1,128)}), f32[32,1,64]{2,1,0:T(1,128)S(1)}, u32[]{:S(2)}, u32[]{:S(2)}) async-start(f32[32,1,64]{2,1,0:T(1,128)} %max_broadcast_in_dim.15), calls=%async_computation.2 | async-start | bytes 32768 | tf_op jit(solution)/shard_map/all_to_all | solution.py:47
Sparse Core Ops, SparseCore 0:
  77.1 152.9 all-gather.1
where the time goes:
time: 298 us
  waiting for transfers between devices  134 us (45%)
  blocking collectives  81.5 us (27%)
  matrix products  40.3 us (14%)
  between operations  13.5 us (5%)
  other arithmetic  12.2 us (4%)
  local copies, waits for them, and re-layouts  9.02 us (3%)
  starting transfers between devices  7.45 us (2%)
    all_gather x1, waiting for transfers between devices, local(): lax.all_gather(query, 'blk', axis=0, tiled=True)  127 us
    all_to_all x1, blocking collectives, local(): lax.all_to_all(outbox.reshape(groups, slots, width), 'grp', split_axis=0,...  59.3 us
    dot_general x1, matrix products, local(): lax.dot_general(query, lax.all_gather(query, 'blk', axis=0, tiled=True),...  40.3 us
    all_gather x1, blocking collectives, local(): lax.all_gather(q_rank, 'blk', axis=0, tiled=True)[None, :] < q_rank[:, None]  11.5 us
    all_to_all x1, blocking collectives, local(): lax.all_to_all(outrank.reshape(groups, slots), 'grp', split_axis=0, conca...  10.7 us
    all_to_all x1, starting transfers between devices, local(): lax.all_to_all(best_local.reshape(groups, slots), 'grp', split_axis=0, co...  7.45 us
    all_to_all x1, waiting for transfers between devices, local(): lax.all_to_all(best_local.reshape(groups, slots), 'grp', split_axis=0, co...  6.93 us
  transfers between devices with their start and end apart: 2, of which 2 were waited for; matrix products, arithmetic and copies ran while one was open for 1% of the time, Pallas kernels for 0%

commit v1 on v0

--- a/solution.py
+++ b/solution.py
@@ -36,7 +36,9 @@
     start_best = jnp.full((local_rows,), -1.0, jnp.float32)
     scores = lax.dot_general(
         query,
-        lax.all_gather(query, "blk", axis=0, tiled=True),
+        jnp.concatenate(
+            lax.all_to_all(jnp.stack([query] * lax.axis_size("blk")), "blk", 0, 0), axis=0
+        ),
         (((1,), (1,)), ((), ())),
         preferred_element_type=jnp.float32,
     )

time: 298 us -> 345 us (1.16)
  blocking collectives: 81.5 us -> 245 us
  waiting for transfers between devices: 134 us -> 7.03 us
  starting transfers between devices: 7.45 us -> 23.1 us
  between operations: 13.5 us -> 0.08 us
  local copies, waits for them, and re-layouts: 9.02 us -> 17.6 us
    all_gather x1, blocking collectives: 11.5 us -> 187 us  [local(): lax.all_gather(q_rank, 'blk', axis=0, tiled=True)[None, :] < q_rank[:, None]]
    all_gather x1 -> x0, waiting for transfers between devices: 127 us -> none  [local(): lax.all_gather(query, 'blk', axis=0, tiled=True)]
    all_to_all x0 -> x2, starting transfers between devices: none -> 15.5 us  [the longest x1 8.59 us: local(): lax.all_to_all(outrank.reshape(groups, slots), 'grp', split_axis=0, conca...]
    all_to_all x1 -> x0, blocking collectives: 10.7 us -> none  [local(): lax.all_to_all(outrank.reshape(groups, slots), 'grp', split_axis=0, conca...]
    another operation x1 -> x2, local copies, waits for them, and re-layouts: 0.01 us -> 5.95 us  [the longest x1 5.95 us: local(): jnp.stack([query] * lax.axis_size('blk'))]
  transfers between devices with their start and end apart: 2 -> 3, of which waited for: 2 -> 1; matrix products, arithmetic and copies ran while one was open for 1% -> 3% of each run, Pallas kernels for 0% -> 0%
where the time goes in v1:
time: 345 us
  blocking collectives  245 us (71%)
  matrix products  40.2 us (12%)
  starting transfers between devices  23.1 us (7%)
  local copies, waits for them, and re-layouts  17.6 us (5%)
  other arithmetic  12.2 us (4%)
  waiting for transfers between devices  7.03 us (2%)
    all_gather x1, blocking collectives, local(): lax.all_gather(q_rank, 'blk', axis=0, tiled=True)[None, :] < q_rank[:, None]  187 us
    all_to_all x1, blocking collectives, local(): lax.all_to_all(outbox.reshape(groups, slots, width), 'grp', split_axis=0,...  58 us
    dot_general x1, matrix products, local(): lax.dot_general(query, jnp.concatenate(lax.all_to_all(jnp.stack([query] *...  40.2 us
    all_to_all x1, starting transfers between devices, local(): lax.all_to_all(outrank.reshape(groups, slots), 'grp', split_axis=0, conca...  8.59 us
    all_to_all x1, starting transfers between devices, local(): lax.all_to_all(best_local.reshape(groups, slots), 'grp', split_axis=0, co...  7.53 us
    all_to_all x1, waiting for transfers between devices, local(): lax.all_to_all(best_local.reshape(groups, slots), 'grp', split_axis=0, co...  7.03 us
    all_to_all x1, starting transfers between devices, local(): lax.all_to_all(jnp.stack([query] * lax.axis_size('blk')), 'blk', 0, 0)  6.96 us
  transfers between devices with their start and end apart: 3, of which 1 were waited for; matrix products, arithmetic and copies ran while one was open for 3% of the time, Pallas kernels for 0%

profile of v1, /device:TPU:1, one launch (start us, length us, event | category | flops | bytes accessed | tf_op | source)
XLA Modules:
  0.0 344.9 jit_solution(10612401520544179014)
XLA Ops:
  0.0 0.7 fusion.9
  0.7 1.2 reduce-window.6
  1.8 0.2 slice_reduce_fusion
  2.1 0.8 fusion.8
  2.9 0.7 compare_select_fusion
  3.6 2.6 scatter_custom_fusion
  6.2 0.7 all_to_all.16
  6.9 8.6 %all-to-all-start = ((s32[32,1,64]{2,1,0:T(1,128)}), s32[32,1,64]{2,1,0:T(1,128)S(1)}, u32[]{:S(2)}, u32[]{:S(2)}) async-start(s32[32,1,64]{2,1,0:T(1,128)} %all_to_all.16), calls=%async_computation | async-start | bytes 32768 | tf_op jit(solution)/shard_map/all_to_all | solution.py:29
  15.5 1.5 fusion
  17.0 6.0 %scatter_custom_fusion.1 = bf16[2048,1024]{1,0:T(8,128)(2,1)} fusion(s32[512]{0:T(512)S(1)} %bitcast.34, bf16[]{:T(256)} %constant.4.clone.1, bf16[512,1024]{1,0:T(8,128)(2,1)} %param.3, f32[512]{0:T(512)S(1)} %add_sqrt_fusion), kind=kCustom, calls=%fused_computation.8 | custom fusion | flops 1572864 | bytes 5244930 | tf_op jit(solution)/shard_map/scatter | solution.py:23
  22.9 58.0 %all_to_all.25 = bf16[32,64,1024]{2,1,0:T(8,128)(2,1)S(1)} all-to-all(bf16[32,64,1024]{2,1,0:T(8,128)(2,1)} %bitcast.30), channel_id=1, replica_groups=mesh['grp'=32,'blk'=4] {'grp'}, dimensions={0} | all-to-all | bytes 8388608 | tf_op jit(solution)/shard_map/all_to_all | solution.py:26
  81.0 2.0 copy-done
  83.0 5.9 %stack.3 = bf16[4,2048,1024]{2,1,0:T(8,128)(2,1)} broadcast(bf16[2048,1024]{1,0:T(8,128)(2,1)S(1)} %bitcast.28), dimensions={1,2} | broadcast | bytes 20971520 | tf_op jit(solution)/shard_map/stack | solution.py:40
  88.9 7.0 %all-to-all-start.2 = ((bf16[4,2048,1024]{2,1,0:T(8,128)(2,1)}), bf16[4,2048,1024]{2,1,0:T(8,128)(2,1)}, u32[]{:S(2)}, u32[]{:S(2)}) async-start(bf16[4,2048,1024]{2,1,0:T(8,128)(2,1)} %stack.3), calls=%async_computation.2 | async-start | bytes 33554432 | tf_op jit(solution)/shard_map/all_to_all | solution.py:40
  95.9 0.5 broadcast.59
  96.4 0.7 reduce.8
  97.2 186.7 %all_gather.3 = s32[8192]{0:T(1024)S(1)} all-gather(s32[2048]{0:T(1024)S(1)} %reshape.66), channel_id=1, replica_groups=mesh['grp'=32,'blk'=4] {'blk'}, dimensions={0}, use_global_device_ids=true | all-gather | bytes 40960 | tf_op jit(solution)/shard_map/all_gather | solution.py:45
  283.9 40.2 %select_reduce_fusion = f32[2048]{0:T(1024)S(1)} fusion(bf16[2048,1024]{1,0:T(8,128)(2,1)} %bitcast.29, bf16[8192,1024]{1,0:T(8,128)(2,1)} %bitcast.7, s32[8192]{0:T(1024)S(1)} %all_gather.3, s32[2048]{0:T(1024)S(1)} %reshape.66), kind=kOutput, calls=%fused_computation.3 | convolution fusion | flops 34410070016 | bytes 21020672 | tf_op jit(solution)/shard_map/dot_general | solution.py:37
  324.1 0.7 max_broadcast_in_dim.15
  324.8 7.5 %all-to-all-start.3 = ((f32[32,1,64]{2,1,0:T(1,128)}), f32[32,1,64]{2,1,0:T(1,128)S(1)}, u32[]{:S(2)}, u32[]{:S(2)}) async-start(f32[32,1,64]{2,1,0:T(1,128)} %max_broadcast_in_dim.15), calls=%async_computation.3 | async-start | bytes 32768 | tf_op jit(solution)/shard_map/all_to_all | solution.py:49
  332.3 7.0 %all-to-all-done.3 = f32[32,1,64]{2,1,0:T(1,128)S(1)} async-done(((f32[32,1,64]{2,1,0:T(1,128)}), f32[32,1,64]{2,1,0:T(1,128)S(1)}, u32[]{:S(2)}, u32[]{:S(2)}) %all-to-all-start.3) | async-done | bytes 8224 | tf_op jit(solution)/shard_map/all_to_all | solution.py:49
  339.4 0.5 broadcast.60
  339.9 0.7 reduce.9
  340.6 4.3 %gather_fusion = f32[512]{0:T(512)} fusion(f32[2048]{0:T(1024)S(1)} %reshape.70, s32[1024]{0:T(1024)S(1)} %pad_clamp_fusion), kind=kCustom, calls=%fused_computation | custom fusion | bytes 6144 | tf_op jit(solution)/shard_map/gather | solution.py:52
  (10 shorter events, 0.2 us)
Async XLA Ops:
  6.9 16.1 %all-to-all-start = ((s32[32,1,64]{2,1,0:T(1,128)}), s32[32,1,64]{2,1,0:T(1,128)S(1)}, u32[]{:S(2)}, u32[]{:S(2)}) async-start(s32[32,1,64]{2,1,0:T(1,128)} %all_to_all.16), calls=%async_computation | async-start | bytes 32768 | tf_op jit(solution)/shard_map/all_to_all | solution.py:29
  80.9 2.0 copy-start
  88.9 194.9 %all-to-all-start.2 = ((bf16[4,2048,1024]{2,1,0:T(8,128)(2,1)}), bf16[4,2048,1024]{2,1,0:T(8,128)(2,1)}, u32[]{:S(2)}, u32[]{:S(2)}) async-start(bf16[4,2048,1024]{2,1,0:T(8,128)(2,1)} %stack.3), calls=%async_computation.2 | async-start | bytes 33554432 | tf_op jit(solution)/shard_map/all_to_all | solution.py:40
  324.8 14.6 %all-to-all-start.3 = ((f32[32,1,64]{2,1,0:T(1,128)}), f32[32,1,64]{2,1,0:T(1,128)S(1)}, u32[]{:S(2)}, u32[]{:S(2)}) async-start(f32[32,1,64]{2,1,0:T(1,128)} %max_broadcast_in_dim.15), calls=%async_computation.3 | async-start | bytes 32768 | tf_op jit(solution)/shard_map/all_to_all | solution.py:49
